TPU v7x, 512 devices: a whole 4x4x16 slice. The times are simulated.
512 devices in a mesh: feat: 16 (over z), batch: 32 (over y, x, core).
Axes of the slice: x: 4, y: 4, z: 16, core: 2. Of those that a mesh axis runs over, the one named last changes fastest.
Arguments:
- feats: bfloat16 [32, 768, 8192], P('batch', 'feat'), may hold values from -6 to 6
- nbr_one: int32 [32, 15, 1024], P('batch'), may hold values from 0 to 8191
- rel_one: int32 [32, 15, 1024], P('batch'), may hold values from 0 to 4
- w_one: bfloat16 [5, 768, 1024], P(None, 'feat'), may hold values from -0.09375 to 0.09375
- owner_two: int32 [32, 1024, 10, 1], P('batch'), may hold values from 0 to 31; in each aligned block of 640 rows (0 to 639, 640 to 1279, ..., all dimensions but the last counted through in order) at most 40 rows name the same one
- local_two: int32 [32, 1024, 10], P('batch'), may hold values from 0 to 63
- rel_two: int32 [32, 1024, 10], P('batch'), may hold values from 0 to 4
- w_two: bfloat16 [5, 1024, 1024], P(None, 'feat'), may hold values from -0.078125 to 0.078125
Outputs:
- hidden_two: bfloat16 [32, 1024, 1024], P('batch', 'feat')
Inputs may be any that keep to these rules, and one draw needn't show every extreme that they name: `owner_two`: every neighbour of destination j lies in the block of rows (j // 64) * 64 to (j // 64) * 64 + 63 of its mini-batch; among the 640 edges of each aligned block of 64 destinations, no mini-batch is named more than 40 times. `rel_one`: the value 4 marks an empty slot. `rel_two`: the value 4 marks an empty slot.
All inputs are finite; a program needn't handle non-finite values.
Results may differ from a plain program's by a relative error of at most 0.025.
Values may be sent and summed in bfloat16 or wider, within the bound.
A program may use at most 64 MiB of HBM per device.

v0:
```python
import jax
import jax.numpy as jnp
from jax import lax
from jax.sharding import PartitionSpec as P

RELATIONS = 4
FANOUT_TWO = 10
ROWS = 64


def relation_counts(relation_ids, along):
    counted = [
        jnp.maximum(jnp.sum((relation_ids == relation).astype(jnp.int32), axis=along), 1)
        for relation in range(RELATIONS)
    ]
    return jnp.stack(counted).astype(jnp.float32)


def first_means(columns, neighbours, relation_ids):
    dest_rows = neighbours.shape[1]
    picked = jnp.take(columns, neighbours, axis=1)
    counter = relation_counts(relation_ids, 0)
    slabs = [columns[:, :dest_rows]]
    for relation in range(RELATIONS):
        chosen = relation_ids == relation
        summed = jnp.sum(
            jnp.where(chosen[None], picked, jnp.zeros((), picked.dtype)), axis=1, dtype=jnp.float32
        )
        slabs.append((summed / counter[relation][None, :]).astype(jnp.bfloat16))
    return jnp.stack(slabs)


def place_requests(owner_flat, within_flat, batches, capacity):
    edges = owner_flat.shape[0]
    matches = (owner_flat[:, None] == jnp.arange(batches, dtype=jnp.int32)[None, :]).astype(
        jnp.bfloat16
    )
    order = jnp.arange(edges, dtype=jnp.int32)
    earlier = (order[None, :] < order[:, None]).astype(jnp.bfloat16)
    before = jnp.dot(earlier, matches, preferred_element_type=jnp.float32)
    slot_index = jnp.sum(before * matches.astype(jnp.float32), axis=1).astype(jnp.int32)
    places = (slot_index[:, None] == jnp.arange(capacity, dtype=jnp.int32)[None, :]).astype(
        jnp.float32
    )
    valued = matches.astype(jnp.float32) * within_flat.astype(jnp.float32)[:, None]
    request = jnp.einsum("eb,ec->bc", valued, places, precision=lax.Precision.HIGHEST).astype(
        jnp.int32
    )
    return (slot_index, request)


def body(feats, nbr_one, rel_one, w_one, owner_two, local_two, rel_two, w_two):
    columns = feats[0]
    slabs = first_means(columns, nbr_one[0], rel_one[0])
    batches = lax.axis_size("batch")
    capacity = (2 * ROWS * FANOUT_TWO + batches - 1) // batches
    span = batches * capacity
    labels = jnp.arange(RELATIONS * span, dtype=jnp.int32)
    owners = owner_two[0, :, :, 0]
    within = local_two[0]
    relation_ids = rel_two[0]
    portion = slabs
    hidden_one = jax.nn.relu(
        lax.psum_scatter(
            jnp.einsum("sfd,sfh->dh", portion, w_one, preferred_element_type=jnp.float32).astype(
                jnp.bfloat16
            ),
            "feat",
            scatter_dimension=0,
            tiled=True,
        ).astype(jnp.float32)
    ).astype(jnp.bfloat16)
    offset = lax.axis_index("feat") * ROWS
    mine_owner = lax.dynamic_slice_in_dim(owners, offset, ROWS, 0).reshape(-1)
    mine_within = lax.dynamic_slice_in_dim(within, offset, ROWS, 0).reshape(-1)
    mine_ids = lax.dynamic_slice_in_dim(relation_ids, offset, ROWS, 0)
    slot_index, request = place_requests(mine_owner, mine_within, batches, capacity)
    onehot = (
        lax.all_to_all(request, "batch", split_axis=0, concat_axis=0, tiled=True)[..., None]
        == jnp.arange(ROWS, dtype=jnp.int32)
    ).astype(jnp.bfloat16)
    replies = jnp.einsum(
        "bmr,rh->bmh", onehot, hidden_one, preferred_element_type=jnp.float32
    ).astype(jnp.bfloat16)
    arrived = lax.all_to_all(replies, "batch", split_axis=0, concat_axis=0, tiled=True)
    flat = arrived.reshape(span, arrived.shape[2])
    positions = (mine_owner * capacity + slot_index).reshape(ROWS, FANOUT_TWO)
    keys = mine_ids * span + positions
    table = jnp.zeros((ROWS, RELATIONS * span), jnp.bfloat16)
    for slot in range(FANOUT_TWO):
        table = table + (keys[:, slot][:, None] == labels[None, :]).astype(jnp.bfloat16)
    table = table.reshape(ROWS, RELATIONS, span)
    summed = jnp.einsum("drc,ch->rdh", table, flat, preferred_element_type=jnp.float32)
    counter = relation_counts(mine_ids, 1)
    means = (summed / counter[:, :, None]).astype(jnp.bfloat16)
    inputs = jnp.concatenate([hidden_one[None], means], axis=0)
    block_size = w_two.shape[1]
    shard_piece = lax.all_gather(w_two, "feat", axis=1, tiled=True)
    amount = shard_piece.shape[1]
    groups = amount // block_size
    portion = inputs
    portion = portion.reshape(portion.shape[0], portion.shape[1], groups, block_size)
    weights = shard_piece.reshape(shard_piece.shape[0], groups, block_size, shard_piece.shape[2])
    products = jnp.einsum("sdgk,sgkh->gdh", portion, weights, preferred_element_type=jnp.float32)
    rounded = lax.optimization_barrier(products.astype(jnp.bfloat16)).astype(jnp.float32)
    running = jnp.sum(rounded, axis=0)
    result = jax.nn.relu(running).astype(jnp.bfloat16)
    return result[None]


def solution(mesh):
    in_specs = (
        P("batch", "feat", None),
        P("batch", None, None),
        P("batch", None, None),
        P(None, "feat", None),
        P("batch", None, None, None),
        P("batch", None, None),
        P("batch", None, None),
        P(None, "feat", None),
    )
    out_specs = P("batch", "feat", None)
    return jax.shard_map(body, mesh=mesh, in_specs=in_specs, out_specs=out_specs, check_vma=False)
```

profile of v0, /device:TPU:1, one launch (start us, length us, event | category | flops | bytes accessed | tf_op | source)
XLA Modules:
  0.0 303.7 jit_solution(5919092703397115076)
XLA Ops:
  6.5 0.0 copy-start
  6.5 0.0 reduce-scatter.2.cloned.1.call-start
  6.5 0.9 compare_select_fusion
  7.5 0.9 compare_and_fusion
  8.4 1.1 broadcast_compare_fusion.1
  9.4 1.1 convert_reduce_fusion.8
  10.6 2.0 copy.27
  12.6 0.9 fusion.45
  13.5 53.9 %gather_fusion = bf16[15360,48]{1,0:T(8,128)(2,1)} fusion(bf16[48,8192]{0,1:T(8,128)(2,1)S(1)} %copy.27, s32[15360]{0:T(1024)S(1)} %broadcast_clamp_fusion), kind=kCustom, calls=%fused_computation | custom fusion | bytes 3010560 | tf_op jit(solution)/shard_map/jit(_take)/gather | solution.py:21
  67.5 13.3 %convert_reduce_fusion = (f32[1024,48]{1,0:T(8,128)S(1)}, f32[1024,48]{1,0:T(8,128)S(1)}, f32[1024,48]{1,0:T(8,128)S(1)}, f32[1024,48]{1,0:T(8,128)S(1)}) fusion(pred[15,1024]{1,0:T(8,128)(4,1)S(1)} %get-tuple-element.41, bf16[15,1024,48]{2,1,0:T(8,128)(2,1)} %bitcast.106, pred[15,1024]{1,0:T(8,128)(4,1)S(1)} %compare_and_fusion, ...), kind=kLoop, calls=%fused_computation.3 | loop fusion | flops 9388032 | bytes 2337792 | tf_op jit(solution)/shard_map/reduce_sum | solution.py:26
  80.8 0.2 copy.28
  81.1 0.2 copy.29
  81.3 0.2 copy.30
  81.4 0.2 copy.31
  81.7 0.0 copy-done
  81.7 2.0 bitcast_convert_fusion.1
  83.8 0.0 reduce-scatter.2.cloned.1.call-update
  83.8 0.0 all-gather.2.cloned.1.call-start
  83.9 0.7 all-gather.2.cloned.1.call-update
  84.6 0.8 constant_dynamic-slice_fusion.1
  85.3 0.1 copy.45
  85.4 0.1 eq.341
  85.6 0.3 fusion.11
  85.9 0.8 dynamic-slice_convert_fusion
  86.7 0.1 copy.33
  86.8 0.1 convert_element_type.261
  86.9 0.3 convolution_convert_fusion.1
  87.3 16.5 %all_to_all.14 = s32[32,1,40]{2,1,0:T(1,128)S(1)} all-to-all(s32[32,1,40]{2,1,0:T(1,128)S(1)} %bitcast.116), channel_id=1, replica_groups=mesh['feat'=16,'batch'=32] {'batch'}, dimensions={0} | all-to-all | bytes 10240 | tf_op jit(solution)/shard_map/all_to_all | solution.py:79
  103.8 48.4 %reduce-scatter.2.cloned.1.call-done = bf16[64,1024]{1,0:T(8,128)(2,1)} async-done(((bf16[1024,1024]{1,0:T(8,128)(2,1)}), bf16[64,1024]{1,0:T(8,128)(2,1)}) %reduce-scatter.2.cloned.1.call-update) | async-done | bytes 131088 | tf_op jit(solution)/shard_map/reduce_scatter | solution.py:64
  152.2 3.3 %convolution_convert_fusion = bf16[32,40,1024]{2,1,0:T(8,128)(2,1)} fusion(s32[32,40]{1,0:T(8,128)S(1)} %bitcast.111, bf16[64,1024]{1,0:T(8,128)(2,1)} %reduce-scatter.2.cloned.1.call-done), kind=kOutput, calls=%fused_computation.11 | convolution fusion | flops 169361408 | bytes 2757632 | tf_op jit(solution)/shard_map/bmr,rh->bmh/dot_general | solution.py:82
  155.5 0.0 copy-start.1
  155.5 18.1 %all-to-all-start.1 = ((bf16[32,40,1024]{2,1,0:T(8,128)(2,1)}), bf16[32,40,1024]{2,1,0:T(8,128)(2,1)S(1)}, u32[]{:S(2)}, u32[]{:S(2)}) async-start(bf16[32,40,1024]{2,1,0:T(8,128)(2,1)} %convolution_convert_fusion), calls=%async_computation.2 | async-start | bytes 5242880 | tf_op jit(solution)/shard_map/all_to_all | solution.py:85
  173.6 0.1 convert_element_type.265
  173.7 0.1 copy.46
  173.8 0.1 convert_reduce_fusion.12
  174.1 1.0 slice_reduce_fusion.9
  175.0 0.0 copy-done.1
  175.1 0.2 concatenate.12
  175.3 0.8 copy.36
  176.1 31.1 %all-to-all-done.1 = bf16[32,40,1024]{2,1,0:T(8,128)(2,1)S(1)} async-done(((bf16[32,40,1024]{2,1,0:T(8,128)(2,1)}), bf16[32,40,1024]{2,1,0:T(8,128)(2,1)S(1)}, u32[]{:S(2)}, u32[]{:S(2)}) %all-to-all-start.1) | async-done | bytes 2621472 | tf_op jit(solution)/shard_map/all_to_all | solution.py:85
  207.2 3.2 %fusion.9 = bf16[4,64,1024]{2,1,0:T(8,128)(2,1)} fusion(bf16[1280,1024,1]{1,0,2:T(8,128)(2,1)S(1)} %bitcast.107, s32[4,1280]{1,0:T(4,128)S(1)} %multiply_add_fusion, s32[64]{0:T(128)S(1)} %get-tuple-element.18, s32[64]{0:T(128)S(1)} %get-tuple-element.19, s32[64]{0:T(128)S(1)} %get-tuple-element.20, s32[64]{0:T(128)S(1)} %get-tuple-element.21, ...), kind=kOutput, calls=%fused_computation.29 | convolution fusion | flops 684720128 | bytes 3169792 | tf_op jit(solution)/shard_map/drc,ch->rdh/dot_general | solution.py:93
  210.3 1.8 concatenate.13
  212.2 0.3 copy.37
  212.4 77.0 %all-gather.2.cloned.1.call-done = bf16[5,1024,1024]{2,1,0:T(8,128)(2,1)} async-done(((bf16[5,64,1024]{2,1,0:T(8,128)(2,1)}), bf16[5,1024,1024]{2,1,0:T(8,128)(2,1)}) %all-gather.2.cloned.1.call-update) | async-done | bytes 10485776 | tf_op jit(solution)/shard_map/all_gather | solution.py:98
  289.4 0.0 copy-done.2
  289.4 6.3 %bitcast_convert_fusion = bf16[16,64,1024]{2,1,0:T(8,128)(2,1)S(1)} fusion(bf16[5,16,64,1024]{3,2,1,0:T(8,128)(2,1)} %bitcast.121, bf16[4,64,16,64]{3,1,0,2:T(8,128)(2,1)S(1)} %copy.37, bf16[1,64,16,64]{3,1,0,2:T(8,128)(2,1)S(1)} %copy-done.2), kind=kOutput, calls=%fused_computation.7 | convolution fusion | flops 672464896 | bytes 13238272 | tf_op jit(solution)/shard_map/sdgk,sgkh->gdh/dot_general | solution.py:104
  295.8 0.3 convert_reduce_fusion.4
  296.1 0.7 fusion.39
  (21 shorter events, 0.3 us)
Async XLA Ops:
  6.5 75.2 %copy-start = (bf16[5,48,1024]{2,1,0:T(8,128)(2,1)S(1)}, bf16[5,48,1024]{2,1,0:T(8,128)(2,1)}, u32[]{:S(2)}) copy-start(bf16[5,48,1024]{2,1,0:T(8,128)(2,1)} %param.11) | copy-start | bytes 1474564
  6.5 145.7 %reduce-scatter.2.cloned.1.call-start = ((), (), s32[]{:S(2)}) async-start(), calls=%async_computation.3 | async-start | bytes 2228224 | tf_op jit(solution)/shard_map/reduce_scatter | solution.py:64
  83.8 205.6 %all-gather.2.cloned.1.call-start = ((), (), s32[]{:S(2)}) async-start(), calls=%async_computation.4 | async-start | bytes 11141120 | tf_op jit(solution)/shard_map/all_gather | solution.py:98
  155.5 19.5 %copy-start.1 = (bf16[64,1024]{1,0:T(8,128)(2,1)S(1)}, bf16[64,1024]{1,0:T(8,128)(2,1)}, u32[]{:S(2)}) copy-start(bf16[64,1024]{1,0:T(8,128)(2,1)} %reduce-scatter.2.cloned.1.call-done) | copy-start | bytes 393220
  155.5 51.7 %all-to-all-start.1 = ((bf16[32,40,1024]{2,1,0:T(8,128)(2,1)}), bf16[32,40,1024]{2,1,0:T(8,128)(2,1)S(1)}, u32[]{:S(2)}, u32[]{:S(2)}) async-start(bf16[32,40,1024]{2,1,0:T(8,128)(2,1)} %convolution_convert_fusion), calls=%async_computation.2 | async-start | bytes 5242880 | tf_op jit(solution)/shard_map/all_to_all | solution.py:85
  210.3 79.1 %copy-start.2 = (bf16[1,64,16,64]{3,1,0,2:T(8,128)(2,1)S(1)}, bf16[1,64,16,64]{3,1,0,2:T(8,128)(2,1)}, u32[]{:S(2)}) copy-start(bf16[1,64,16,64]{3,1,0,2:T(8,128)(2,1)} %copy.36) | copy-start | bytes 393220
Sparse Core Ops, SparseCore 0:
  83.9 68.2 reduce-scatter.1
  154.3 135.1 all-gather.1
where the time goes:
time: 304 us
  waiting for transfers between devices  157 us (52%)
  local copies, waits for them, and re-layouts  63.1 us (21%)
  other arithmetic  19.5 us (6%)
  starting transfers between devices  18.1 us (6%)
  blocking collectives  16.5 us (5%)
  matrix products  15.5 us (5%)
  between operations  13.7 us (5%)
    all_gather x1, waiting for transfers between devices, body(): shard_piece = lax.all_gather(w_two, 'feat', axis=1, tiled=True)  77 us
    gather x1, local copies, waits for them, and re-layouts, first_means(): picked = jnp.take(columns, neighbours, axis=1)  53.9 us
    reduce_scatter x1, waiting for transfers between devices, body(): lax.psum_scatter(jnp.einsum('sfd,sfh->dh', portion, w_one, preferred_elem...  48.4 us
    all_to_all x1, waiting for transfers between devices, body(): lax.all_to_all(replies, 'batch', split_axis=0, concat_axis=0, tiled=True)  31.1 us
    all_to_all x1, starting transfers between devices, body(): lax.all_to_all(replies, 'batch', split_axis=0, concat_axis=0, tiled=True)  18.1 us
    all_to_all x1, blocking collectives, body(): lax.all_to_all(request, 'batch', split_axis=0, concat_axis=0, tiled=True)  16.5 us
    reduce_sum x1, other arithmetic, first_means(): jnp.sum(jnp.where(chosen[None], picked, jnp.zeros((), picked.dtype)), axi...  13.3 us
    dot_general x1, matrix products, body(): jnp.einsum('sdgk,sgkh->gdh', portion, weights, preferred_element_type=jnp...  6.34 us
  transfers between devices with their start and end apart: 3, of which 3 were waited for; matrix products, arithmetic and copies ran while one was open for 4% of the time, Pallas kernels for 0%

commit v1 on v0

--- a/solution.py
+++ b/solution.py
@@ -95,7 +95,10 @@
     means = (summed / counter[:, :, None]).astype(jnp.bfloat16)
     inputs = jnp.concatenate([hidden_one[None], means], axis=0)
     block_size = w_two.shape[1]
-    shard_piece = lax.all_gather(w_two, "feat", axis=1, tiled=True)
+    size = lax.axis_size("feat")
+    tiles = jnp.stack([w_two for _ in range(size)])
+    tiles = lax.all_to_all(tiles, "feat", split_axis=0, concat_axis=0)
+    shard_piece = jnp.concatenate(tiles, axis=1)
     amount = shard_piece.shape[1]
     groups = amount // block_size
     portion = inputs

time: 304 us -> 683 us (2.25)
  waiting for transfers between devices: 157 us -> 493 us
  blocking collectives: 16.5 us -> 68.6 us
  starting transfers between devices: 18.1 us -> 8.47 us
    all_to_all x1, waiting for transfers between devices: 31.1 us -> 444 us  [body(): tiles = lax.all_to_all(tiles, 'feat', split_axis=0, concat_axis=0)]
    all_gather x1 -> x0, waiting for transfers between devices: 77 us -> none  [body(): shard_piece = lax.all_gather(w_two, 'feat', axis=1, tiled=True)]
    all_to_all x0 -> x1, blocking collectives: none -> 52 us  [body(): lax.all_to_all(replies, 'batch', split_axis=0, concat_axis=0, tiled=True)]
    all_to_all x1, starting transfers between devices: 18.1 us -> 8.47 us  [body(): tiles = lax.all_to_all(tiles, 'feat', split_axis=0, concat_axis=0)]
  transfers between devices with their start and end apart: 3 -> 2, of which waited for: 3 -> 2; matrix products, arithmetic and copies ran while one was open for 4% -> 1% of each run, Pallas kernels for 0% -> 0%
where the time goes in v1:
time: 683 us; the launch traced here: 682 us
  waiting for transfers between devices  493 us (72%)
  local copies, waits for them, and re-layouts  68.6 us (10%)
  blocking collectives  68.6 us (10%)
  other arithmetic  16.2 us (2%)
  between operations  13.7 us (2%)
  matrix products  13.3 us (2%)
  starting transfers between devices  8.47 us (1%)
    all_to_all x1, waiting for transfers between devices, body(): tiles = lax.all_to_all(tiles, 'feat', split_axis=0, concat_axis=0)  444 us
    gather x1, local copies, waits for them, and re-layouts, first_means(): picked = jnp.take(columns, neighbours, axis=1)  53.9 us
    all_to_all x1, blocking collectives, body(): lax.all_to_all(replies, 'batch', split_axis=0, concat_axis=0, tiled=True)  52 us
    reduce_scatter x1, waiting for transfers between devices, body(): lax.psum_scatter(jnp.einsum('sfd,sfh->dh', portion, w_one, preferred_elem...  49.1 us
    all_to_all x1, blocking collectives, body(): lax.all_to_all(request, 'batch', split_axis=0, concat_axis=0, tiled=True)  16.5 us
  transfers between devices with their start and end apart: 2, of which 2 were waited for; matrix products, arithmetic and copies ran while one was open for 1% of the time, Pallas kernels for 0%

profile of v1, /device:TPU:1, one launch (start us, length us, event | category | flops | bytes accessed | tf_op | source)
XLA Modules:
  0.0 682.1 jit_solution(4577967965146160522)
XLA Ops:
  6.5 0.0 copy-start
  6.5 0.0 reduce-scatter.2.cloned.1.call-start
  6.5 1.0 fusion.45
  7.5 2.0 copy.25
  9.5 0.0 copy-done.4
  9.5 0.1 compare_select_fusion
  9.6 0.0 copy-done.3
  9.6 0.3 broadcast_compare_fusion.1
  9.9 0.3 convert_reduce_fusion.8
  10.2 53.9 %gather_fusion = bf16[15360,48]{1,0:T(8,128)(2,1)} fusion(bf16[48,8192]{0,1:T(8,128)(2,1)S(1)} %copy.25, s32[15360]{0:T(1024)S(1)} %broadcast_clamp_fusion), kind=kCustom, calls=%fused_computation | custom fusion | bytes 3010560 | tf_op jit(solution)/shard_map/jit(_take)/gather | solution.py:21
  64.2 13.3 %convert_reduce_fusion = (f32[1024,48]{1,0:T(8,128)S(1)}, f32[1024,48]{1,0:T(8,128)S(1)}, f32[1024,48]{1,0:T(8,128)S(1)}, f32[1024,48]{1,0:T(8,128)S(1)}) fusion(pred[15,1024]{1,0:T(8,128)(4,1)S(1)} %get-tuple-element.41, bf16[15,1024,48]{2,1,0:T(8,128)(2,1)} %bitcast.110, pred[15,1024]{1,0:T(8,128)(4,1)S(1)} %compare_and_fusion, ...), kind=kLoop, calls=%fused_computation.3 | loop fusion | flops 9388032 | bytes 2337792 | tf_op jit(solution)/shard_map/reduce_sum | solution.py:26
  77.6 0.2 copy.26
  77.8 0.2 copy.27
  78.0 0.2 copy.28
  78.2 0.2 copy.29
  78.5 0.0 copy-done
  78.5 2.1 bitcast_convert_fusion.1
  80.6 0.0 reduce-scatter.2.cloned.1.call-update
  80.6 0.8 constant_dynamic-slice_fusion.1
  81.4 0.1 copy.42
  81.5 0.1 eq.341
  81.6 0.3 fusion.11
  81.9 0.8 dynamic-slice_convert_fusion
  82.7 0.1 copy.31
  82.8 0.1 convert_element_type.261
  83.0 0.3 convolution_convert_fusion.1
  83.3 16.5 %all_to_all.19 = s32[32,1,40]{2,1,0:T(1,128)S(1)} all-to-all(s32[32,1,40]{2,1,0:T(1,128)S(1)} %bitcast.120), channel_id=1, replica_groups=mesh['feat'=16,'batch'=32] {'batch'}, dimensions={0} | all-to-all | bytes 10240 | tf_op jit(solution)/shard_map/all_to_all | solution.py:79
  99.8 49.1 %reduce-scatter.2.cloned.1.call-done = bf16[64,1024]{1,0:T(8,128)(2,1)} async-done(((bf16[1024,1024]{1,0:T(8,128)(2,1)}), bf16[64,1024]{1,0:T(8,128)(2,1)}) %reduce-scatter.2.cloned.1.call-update) | async-done | bytes 131088 | tf_op jit(solution)/shard_map/reduce_scatter | solution.py:64
  148.9 1.8 convolution_convert_fusion
  150.7 0.0 copy-start.1
  150.7 52.0 %all_to_all.20 = bf16[32,40,1024]{2,1,0:T(8,128)(2,1)S(1)} all-to-all(bf16[32,40,1024]{2,1,0:T(8,128)(2,1)S(1)} %convolution_convert_fusion), channel_id=1, replica_groups=mesh['feat'=16,'batch'=32] {'batch'}, dimensions={0} | all-to-all | bytes 5242880 | tf_op jit(solution)/shard_map/all_to_all | solution.py:85
  202.8 0.0 copy-done.1
  202.8 5.2 stack.14
  208.0 8.5 %all-to-all-start.2 = ((bf16[16,5,64,1024]{3,2,1,0:T(8,128)(2,1)}), bf16[16,5,64,1024]{3,2,1,0:T(8,128)(2,1)}, u32[]{:S(2)}, u32[]{:S(2)}) async-start(bf16[16,5,64,1024]{3,2,1,0:T(8,128)(2,1)} %stack.14), calls=%async_computation.3 | async-start | bytes 20971520 | tf_op jit(solution)/shard_map/all_to_all | solution.py:100
  216.5 0.1 convert_element_type.265
  216.6 0.1 copy.43
  216.7 0.1 convert_reduce_fusion.12
  216.9 0.4 slice_reduce_fusion.9
  217.3 0.0 copy-done.2
  217.3 0.9 concatenate.12
  218.2 1.0 copy.34
  219.2 2.5 fusion.9
  221.7 1.8 concatenate.13
  223.5 0.3 copy.35
  223.7 444.2 %all-to-all-done.2 = bf16[16,5,64,1024]{3,2,1,0:T(8,128)(2,1)} async-done(((bf16[16,5,64,1024]{3,2,1,0:T(8,128)(2,1)}), bf16[16,5,64,1024]{3,2,1,0:T(8,128)(2,1)}, u32[]{:S(2)}, u32[]{:S(2)}) %all-to-all-start.2) | async-done | bytes 10485792 | tf_op jit(solution)/shard_map/all_to_all | solution.py:100
  667.9 6.3 bitcast_convert_fusion
  674.3 0.3 convert_reduce_fusion.4
  674.6 0.7 fusion.39
  (24 shorter events, 0.3 us)
Async XLA Ops:
  6.5 71.9 %copy-start = (bf16[5,48,1024]{2,1,0:T(8,128)(2,1)S(1)}, bf16[5,48,1024]{2,1,0:T(8,128)(2,1)}, u32[]{:S(2)}) copy-start(bf16[5,48,1024]{2,1,0:T(8,128)(2,1)} %param.11) | copy-start | bytes 1474564
  6.5 3.0 copy-start.4
  6.5 3.1 copy-start.3
  6.5 142.4 %reduce-scatter.2.cloned.1.call-start = ((), (), s32[]{:S(2)}) async-start(), calls=%async_computation.4 | async-start | bytes 2228224 | tf_op jit(solution)/shard_map/reduce_scatter | solution.py:64
  150.7 52.1 %copy-start.1 = (bf16[5,64,1024]{2,1,0:T(8,128)(2,1)S(1)}, bf16[5,64,1024]{2,1,0:T(8,128)(2,1)}, u32[]{:S(2)}) copy-start(bf16[5,64,1024]{2,1,0:T(8,128)(2,1)} %param.15) | copy-start | bytes 1966084
  208.0 9.3 %copy-start.2 = (bf16[64,1024]{1,0:T(8,128)(2,1)S(1)}, bf16[64,1024]{1,0:T(8,128)(2,1)}, u32[]{:S(2)}) copy-start(bf16[64,1024]{1,0:T(8,128)(2,1)} %reduce-scatter.2.cloned.1.call-done) | copy-start | bytes 393220
  208.0 459.9 %all-to-all-start.2 = ((bf16[16,5,64,1024]{3,2,1,0:T(8,128)(2,1)}), bf16[16,5,64,1024]{3,2,1,0:T(8,128)(2,1)}, u32[]{:S(2)}, u32[]{:S(2)}) async-start(bf16[16,5,64,1024]{3,2,1,0:T(8,128)(2,1)} %stack.14), calls=%async_computation.3 | async-start | bytes 20971520 | tf_op jit(solution)/shard_map/all_to_all | solution.py:100
Sparse Core Ops, SparseCore 0:
  80.7 68.1 reduce-scatter.1
